TPU v7x, 256 devices: a whole 4x4x8 slice. The times are simulated.
256 devices in a mesh: vox: 32 (over z, y), col: 8 (over x, core).
Axes of the slice: x: 4, y: 4, z: 8, core: 2. Of those that a mesh axis runs over, the one named last changes fastest.
Arguments:
- start_modes: float32 [128, 131072], P('col', 'vox'), may hold values from -48 to 48
- start_dirs: float32 [128, 131072], P('col', 'vox'), may hold values from -6 to 6
- coupling: float32 [13, 131072], P(None, ('vox', 'col')), may hold values from 0.05 to 1
- relax_class: int32 [131072], P(('vox', 'col')), may hold values from 0 to 3
- relaxivity: float32 [4], replicated, may hold values from 0.5 to 4
Outputs:
- modes: float32 [128, 131072], P('col', 'vox')
- ritz: float32 [128, 128], replicated
All inputs are finite; a program needn't handle non-finite values.
Results may differ from a plain program's by a relative error of at most 0.0003.
Values sent between devices are 32-bit elements; how exact they have to be, the bound alone decides.
A program may use at most 64 MiB of HBM per device.

v0:
```python
import math
import jax
import jax.numpy as jnp
from jax import lax
from jax.sharding import PartitionSpec as P

NX = 256
NZ = 2
HALF = 13
ITERS = 2
QSTEPS = 3
offsets = [
    (a, b, c) for a in (-1, 0, 1) for b in (-1, 0, 1) for c in (-1, 0, 1) if (a, b, c) > (0, 0, 0)
]


def from_behind(block, axis, distance):
    devices = range(lax.axis_size(axis))
    route = [(i - distance, i) for i in devices if i - distance in devices]
    return lax.ppermute(block, axis, route)


def extended_2(block, sides, width):
    for axis, dim in sides:
        count = lax.axis_size(axis)
        forward = [(i, i + 1) for i in range(count - 1)]
        backward = [(target, source) for source, target in forward]
        low = lax.ppermute(
            lax.slice_in_dim(block, block.shape[dim] - width, None, axis=dim), axis, forward
        )
        high = lax.ppermute(lax.slice_in_dim(block, 0, width, axis=dim), axis, backward)
        block = jnp.concatenate([low, block, high], axis=dim)
    return block


def matmul(left, right):
    return jnp.dot(left, right, precision=lax.Precision.HIGHEST, preferred_element_type=jnp.float32)


def lower_solve(lower, rhs):
    return lax.linalg.triangular_solve(lower, rhs, left_side=True, lower=True)


def upper_solve(lower, rhs):
    return lax.linalg.triangular_solve(lower, rhs, left_side=True, lower=True, transpose_a=True)


def symmetric(matrix):
    return 0.5 * (matrix + matrix.T)


def project_pencil(gram_a, gram_b, count):
    sym_a = symmetric(gram_a)
    scales = lax.rsqrt(jnp.diagonal(gram_b) + 1e-06)
    normed_b = scales[:, None] * gram_b * scales[None, :]
    normed_a = scales[:, None] * sym_a * scales[None, :]
    lower = jnp.linalg.cholesky(normed_b)
    half_way = lower_solve(lower, normed_a)
    reduced = lower_solve(lower, half_way.T)
    shift = 2.0 * jnp.max(jnp.sum(jnp.abs(reduced), axis=1))
    iterate = jnp.eye(gram_a.shape[0], count, dtype=jnp.float32)
    for sweep_index in range(QSTEPS):
        iterate = shift * iterate - matmul(reduced, iterate)
        factor = jnp.linalg.cholesky(matmul(iterate.T, iterate))
        iterate = lower_solve(factor, iterate.T).T
    return scales[:, None] * upper_solve(lower, iterate)


def neighbour_sum(padded, coupled):
    rows_y = padded.shape[1] - 2
    rows_z = padded.shape[2] - 2
    rows_x = padded.shape[3] - 2
    total = jnp.zeros((padded.shape[0], rows_y, rows_z, rows_x), jnp.float32)
    for which, (step_y, step_z, step_x) in enumerate(offsets):
        ahead = padded[
            :,
            1 + step_y : 1 + step_y + rows_y,
            1 + step_z : 1 + step_z + rows_z,
            1 + step_x : 1 + step_x + rows_x,
        ]
        behind = padded[
            :,
            1 - step_y : 1 - step_y + rows_y,
            1 - step_z : 1 - step_z + rows_z,
            1 - step_x : 1 - step_x + rows_x,
        ]
        here = coupled[which, 1 : 1 + rows_y, 1 : 1 + rows_z, 1 : 1 + rows_x]
        back = coupled[
            which,
            1 - step_y : 1 - step_y + rows_y,
            1 - step_z : 1 - step_z + rows_z,
            1 - step_x : 1 - step_x + rows_x,
        ]
        total = total + here[None] * ahead
        total = total + back[None] * behind
    return total


def pad_plane(array):
    return jnp.pad(array, ((0, 0), (0, 0), (1, 1), (1, 1)))


def quotient(modes, images):
    total = lax.psum(matmul(modes, images.T), ("vox", "col"))
    return symmetric(total)


def on_device(start_modes, start_dirs, coupling, relax_class, relaxivity):
    local_voxels = coupling.shape[1]
    match = relax_class[:, None] == jnp.arange(relaxivity.shape[0], dtype=jnp.int32)[None, :]
    voxel_rate = jnp.sum(jnp.where(match, relaxivity[None, :], jnp.float32(0.0)), axis=1)
    damping = 1.0 / (1.0 + voxel_rate)
    own_coupling = coupling.reshape(HALF, 1, NZ, NX)
    before = from_behind(own_coupling, ("vox", "col"), 1)
    coupled = pad_plane(
        jnp.concatenate([before, own_coupling, jnp.zeros_like(own_coupling)], axis=1)
    )
    position = lax.axis_index(("vox", "col"))
    device_count = lax.axis_size(("vox", "col"))
    plane = jnp.ones((1, 1, NZ, NX), jnp.float32)
    upper_flag = (position > 0).astype(jnp.float32)
    lower_flag = (position < device_count - 1).astype(jnp.float32)
    unity = pad_plane(jnp.concatenate([upper_flag * plane, plane, lower_flag * plane], axis=1))
    degree = neighbour_sum(unity, coupled).reshape(local_voxels)
    diagonal = degree + voxel_rate

    def operate(field):
        count = field.shape[0]
        shaped = field.reshape(count, 1, NZ, NX)
        extended = extended_2(shaped, ((("vox", "col"), 1),), 1)
        padded = pad_plane(extended)
        return diagonal[None, :] * field - neighbour_sum(padded, coupled).reshape(
            count, local_voxels
        )

    modes, dirs = (
        lax.all_to_all(start_modes, "col", split_axis=1, concat_axis=0, tiled=True),
        lax.all_to_all(start_dirs, "col", split_axis=1, concat_axis=0, tiled=True),
    )
    count = modes.shape[0]
    images = operate(modes)
    dir_images = operate(dirs)
    ritz = quotient(modes, images)
    for iteration in range(ITERS):
        resid = images - matmul(ritz, modes)
        search = resid * damping[None, :]
        search_images = operate(search)
        basis = jnp.concatenate([modes, search, dirs], axis=0)
        basis_images = jnp.concatenate([images, search_images, dir_images], axis=0)
        local_a = matmul(basis, basis_images.T)
        local_b = matmul(basis, basis.T)
        gram_a, gram_b = lax.psum((local_a, local_b), ("vox", "col"))
        coeffs = project_pencil(gram_a, gram_b, count)
        modes = matmul(coeffs.T, basis)
        images = matmul(coeffs.T, basis_images)
        dirs = matmul(coeffs[count:].T, basis[count:])
        dir_images = matmul(coeffs[count:].T, basis_images[count:])
        ritz = quotient(modes, images)
    total_voxels = device_count * local_voxels
    scaled = modes * math.sqrt(total_voxels)
    modes_out = lax.all_to_all(scaled, "col", split_axis=0, concat_axis=1, tiled=True)
    return (modes_out, ritz)


def solution(mesh):
    in_specs = (P("col", "vox"), P("col", "vox"), P(None, ("vox", "col")), P(("vox", "col")), P())
    out_specs = (P("col", "vox"), P())
    return jax.shard_map(
        on_device, mesh=mesh, in_specs=in_specs, out_specs=out_specs, check_vma=False
    )
```

profile of v0, /device:TPU:1, one launch (start us, length us, event | category | flops | bytes accessed | tf_op | source)
XLA Modules:
  0.0 1733.3 jit_solution(11976527018198322847)
XLA Ops:
  8.8 6.6 all-to-all-start
  16.2 3.5 collective-permute-start
  25.2 4.1 all-to-all-start.1
  31.4 3.6 collective-permute-start.1
  36.0 2.9 collective-permute-start.6
  38.9 2.6 collective-permute-start.5
  41.6 2.3 select_maximum_fusion.6
  43.9 4.5 multiply_subtract_fusion.3
  49.6 3.4 select_maximum_fusion.2
  53.1 245.1 %all-reduce.15.cloned.1.call-done = f32[128,128]{0,1:T(8,128)} async-done(((f32[128,128]{0,1:T(8,128)}), f32[128,128]{0,1:T(8,128)}) %all-reduce.15.cloned.1.call-update) | async-done | bytes 65552 | tf_op jit(solution)/shard_map/psum | solution.py:104
  303.3 3.9 collective-permute-start.3
  307.2 5.4 fusion.64
  317.3 4.4 fusion.89
  325.0 256.1 %all-reduce.23.cloned.1.call-done = (f32[384,384]{1,0:T(8,128)}, f32[384,384]{0,1:T(8,128)}) async-done(((f32[384,384]{1,0:T(8,128)}, f32[384,384]{0,1:T(8,128)}), (f32[384,384]{1,0:T(8,128)}, f32[384,384]{0,1:T(8,128)})) %all-reduce.23.cloned.1.call-update) | async-done | bytes 1179664 | tf_op jit(solution)/shard_map/psum | solution.py:152
  581.2 6.6 gather_fusion
  590.4 11.7 cholesky.310
  602.2 9.8 custom-call.40
  614.4 11.7 cholesky.329
  626.2 9.9 custom-call.41
  637.5 11.7 cholesky.348
  652.6 5.9 while.12
  658.5 29.7 %custom-call.47 = f32[3,128,128]{1,2,0:T(8,128)S(1)} custom-call(f32[3,128,128]{2,1,0:T(8,128)S(1)} %get-tuple-element.49), custom_call_target="InvertDiagBlocksLowerTriangular" | custom-call | tf_op jit(solution)/shard_map/triangular_solve/custom-call.8 | solution.py:45
  695.7 11.7 cholesky.361
  708.7 9.8 custom-call.44
  720.8 11.7 cholesky.372
  733.9 9.8 custom-call.45
  745.5 11.9 cholesky.383
  758.7 9.8 custom-call.46
  773.6 237.5 %all-reduce.17.cloned.1.call-done = f32[128,128]{1,0:T(8,128)} async-done(((f32[128,128]{1,0:T(8,128)}), f32[128,128]{1,0:T(8,128)}) %all-reduce.17.cloned.1.call-update) | async-done | bytes 65552 | tf_op jit(solution)/shard_map/psum | solution.py:104
  1015.4 3.6 collective-permute-start.7
  1024.6 4.4 fusion.39
  1031.5 259.7 %all-reduce.21.cloned.1.call-done = (f32[384,384]{1,0:T(8,128)}, f32[384,384]{0,1:T(8,128)}) async-done(((f32[384,384]{1,0:T(8,128)}, f32[384,384]{0,1:T(8,128)}), (f32[384,384]{1,0:T(8,128)}, f32[384,384]{0,1:T(8,128)})) %all-reduce.21.cloned.1.call-update) | async-done | bytes 1179664 | tf_op jit(solution)/shard_map/psum | solution.py:152
  1291.2 6.6 gather_fusion.1
  1300.6 11.7 cholesky.396
  1312.4 9.8 custom-call.48
  1324.5 11.7 cholesky.415
  1336.3 10.2 custom-call.49
  1347.8 11.7 cholesky.434
  1363.5 6.4 while.13
  1369.9 29.7 %custom-call.55 = f32[3,128,128]{1,2,0:T(8,128)S(1)} custom-call(f32[3,128,128]{2,1,0:T(8,128)S(1)} %get-tuple-element.52), custom_call_target="InvertDiagBlocksLowerTriangular" | custom-call | tf_op jit(solution)/shard_map/triangular_solve/custom-call.8 | solution.py:45
  1407.1 11.7 cholesky.447
  1420.1 9.8 custom-call.52
  1432.0 11.7 cholesky.458
  1445.0 9.8 custom-call.53
  1456.7 11.9 cholesky.469
  1470.0 9.8 custom-call.54
  1485.0 7.1 all-to-all-start.2
  1492.1 231.0 %all-reduce.19.cloned.1.call-done = f32[128,128]{1,0:T(8,128)} async-done(((f32[128,128]{1,0:T(8,128)}), f32[128,128]{1,0:T(8,128)}) %all-reduce.19.cloned.1.call-update) | async-done | bytes 65552 | tf_op jit(solution)/shard_map/psum | solution.py:104
  (329 shorter events, 108.3 us)
Async XLA Ops:
  8.8 16.4 all-to-all-start
  16.2 8.8 collective-permute-start
  25.2 10.6 all-to-all-start.1
  29.3 268.9 %all-reduce.15.cloned.1.call-start = ((), (), s32[]{:S(2)}) async-start(), calls=%async_computation.3 | async-start | bytes 131072 | tf_op jit(solution)/shard_map/psum | solution.py:104
  29.5 12.1 collective-permute-start.2
  31.4 10.1 collective-permute-start.1
  35.1 13.3 copy-start.21
  35.1 13.3 copy-start.23
  35.1 13.3 copy-start.25
  35.1 13.3 copy-start.27
  35.2 13.3 copy-start.29
  35.2 13.3 copy-start.31
  35.2 13.3 copy-start.33
  35.8 17.2 copy-start.35
  36.0 12.5 copy-start.15
  36.0 13.6 collective-permute-start.6
  38.9 10.7 collective-permute-start.5
  49.6 531.6 %all-reduce.23.cloned.1.call-start = ((), (), s32[]{:S(2)}) async-start(), calls=%async_computation.7 | async-start | bytes 2359296 | tf_op jit(solution)/shard_map/psum | solution.py:152
  301.3 13.6 copy-start.16
  301.3 13.6 collective-permute-start.4
  303.3 11.6 collective-permute-start.3
  312.6 4.6 copy-start.22
  312.6 4.6 copy-start.24
  312.6 4.6 copy-start.26
  312.6 4.6 copy-start.28
  325.0 686.1 %all-reduce.17.cloned.1.call-start = ((), (), s32[]{:S(2)}) async-start(), calls=%async_computation.4 | async-start | bytes 131072 | tf_op jit(solution)/shard_map/psum | solution.py:104
  581.2 6.6 copy-start.2
  581.2 7.7 copy-start
  590.4 11.7 copy-start.12
  744.1 26.5 %copy-start.7 = (f32[128,512]{1,0:T(8,128)S(1)}, f32[128,512]{1,0:T(8,128)}, u32[]{:S(2)}) copy-start(f32[128,512]{1,0:T(8,128)} %copy-done.6) | copy-start | bytes 786436
  744.1 26.5 %copy-start.9 = (f32[128,512]{1,0:T(8,128)S(1)}, f32[128,512]{1,0:T(8,128)}, u32[]{:S(2)}) copy-start(f32[128,512]{1,0:T(8,128)} %copy-done.8) | copy-start | bytes 786436
  770.2 241.8 %copy-start.37 = (f32[512]{0:T(512)S(1)}, f32[512]{0:T(512)}, u32[]{:S(2)}) copy-start(f32[512]{0:T(512)} %get-tuple-element.163) | copy-start | bytes 6148
  771.3 257.8 %copy-start.4 = (f32[128,512]{1,0:T(8,128)}, f32[128,512]{1,0:T(8,128)S(1)}, u32[]{:S(2)}) copy-start(f32[128,512]{1,0:T(8,128)S(1)} %fusion.13) | copy-start | bytes 786436
  773.1 518.2 %all-reduce.21.cloned.1.call-start = ((), (), s32[]{:S(2)}) async-start(), calls=%async_computation.6 | async-start | bytes 2359296 | tf_op jit(solution)/shard_map/psum | solution.py:152
  773.6 255.6 %copy-start.10 = (f32[128,512]{1,0:T(8,128)}, f32[128,512]{1,0:T(8,128)S(1)}, u32[]{:S(2)}) copy-start(f32[128,512]{1,0:T(8,128)S(1)} %fusion.15) | copy-start | bytes 786436
  1013.5 8.3 collective-permute-start.8
  1015.4 6.9 collective-permute-start.7
  1019.5 9.7 copy-start.17
  1029.2 268.7 %copy-start.19 = (f32[128,512]{1,0:T(8,128)}, f32[128,512]{1,0:T(8,128)S(1)}, u32[]{:S(2)}) copy-start(f32[128,512]{1,0:T(8,128)S(1)} %multiply_subtract_fusion) | copy-start | bytes 786436
  1031.5 691.6 %all-reduce.19.cloned.1.call-start = ((), (), s32[]{:S(2)}) async-start(), calls=%async_computation.5 | async-start | bytes 131072 | tf_op jit(solution)/shard_map/psum | solution.py:104
  1291.2 6.7 copy-start.3
  1291.2 7.7 copy-start.1
  1300.5 11.7 copy-start.13
  1454.8 26.9 %copy-start.11 = (f32[128,512]{1,0:T(8,128)S(1)}, f32[128,512]{1,0:T(8,128)}, u32[]{:S(2)}) copy-start(f32[128,512]{1,0:T(8,128)} %copy-done.10) | copy-start | bytes 786436
  1455.9 27.2 %copy-start.5 = (f32[128,512]{1,0:T(8,128)S(1)}, f32[128,512]{1,0:T(8,128)}, u32[]{:S(2)}) copy-start(f32[128,512]{1,0:T(8,128)} %copy-done.4) | copy-start | bytes 786436
  1455.9 27.2 %copy-start.18 = (f32[128,512]{1,0:T(8,128)S(1)}, f32[128,512]{1,0:T(8,128)}, u32[]{:S(2)}) copy-start(f32[128,512]{1,0:T(8,128)} %copy-done.17) | copy-start | bytes 786436
  1455.9 27.2 %copy-start.20 = (f32[128,512]{1,0:T(8,128)S(1)}, f32[128,512]{1,0:T(8,128)}, u32[]{:S(2)}) copy-start(f32[128,512]{1,0:T(8,128)} %copy-done.19) | copy-start | bytes 786436
  1485.0 240.7 %all-to-all-start.2 = ((f32[8,16,512]{2,1,0:T(8,128)}), f32[8,16,512]{2,1,0:T(8,128)S(1)}, u32[]{:S(2)}, u32[]{:S(2)}) async-start(f32[8,16,512]{2,1,0:T(8,128)} %bitcast.87), calls=%async_computation.2 | async-start | bytes 524288 | tf_op jit(solution)/shard_map/all_to_all | solution.py:161
  (7 other events, 23.2 us)
Sparse Core Ops, SparseCore 0:
  49.7 248.4 all-reduce.14
  325.1 256.0 all-reduce.22
  773.2 237.8 all-reduce.16
  1031.6 259.5 all-reduce.20
  1485.1 237.9 all-reduce.18
where the time goes:
time: 1740 us; the launch traced here: 1730 us
  waiting for transfers between devices  1230 us (71%)
  other arithmetic  348 us (20%)
  matrix products  48.7 us (3%)
  starting transfers between devices  44.1 us (3%)
  local copies, waits for them, and re-layouts  41.4 us (2%)
  between operations  21 us (1%)
    psum x3, waiting for transfers between devices, quotient(): total = lax.psum(matmul(modes, images.T), ('vox', 'col'))  714 us
    psum x2, waiting for transfers between devices, on_device(): gram_a, gram_b = lax.psum((local_a, local_b), ('vox', 'col'))  516 us
    another operation x21, other arithmetic, project_pencil(): lower = jnp.linalg.cholesky(normed_b)  114 us
    another operation x18, other arithmetic, project_pencil(): factor = jnp.linalg.cholesky(matmul(iterate.T, iterate))  74.7 us
    another operation x12, other arithmetic, lower_solve(): return lax.linalg.triangular_solve(lower, rhs, left_side=True, lower=True)  62.8 us
    another operation x5, other arithmetic, upper_solve(): lax.linalg.triangular_solve(lower, rhs, left_side=True, lower=True, trans...  59.5 us
  transfers between devices with their start and end apart: 17, of which 6 were waited for; matrix products, arithmetic and copies ran while one was open for 2% of the time, Pallas kernels for 0%

commit v1 on v0

--- a/solution.py
+++ b/solution.py
@@ -101,7 +101,9 @@
 
 
 def quotient(modes, images):
-    total = lax.psum(matmul(modes, images.T), ("vox", "col"))
+    own = matmul(modes, images.T)
+    parts = lax.all_gather(own, ("vox", "col"))
+    total = jnp.sum(parts, axis=0)
     return symmetric(total)
 
 

time: 1740 us -> 1430 us (0.82)
  waiting for transfers between devices: 1230 us -> 890 us
  other arithmetic: 348 us -> 369 us
    psum x3 -> x0, waiting for transfers between devices: 714 us -> none  [quotient(): total = lax.psum(matmul(modes, images.T), ('vox', 'col'))]
    all_gather x0 -> x3, waiting for transfers between devices: none -> 352 us  [quotient(): parts = lax.all_gather(own, ('vox', 'col'))]
    reduce_sum x0 -> x3, other arithmetic: none -> 21.2 us  [quotient(): total = jnp.sum(parts, axis=0)]
  transfers between devices with their start and end apart: 17 -> 16, of which waited for: 6 -> 12; matrix products, arithmetic and copies ran while one was open for 2% -> 2% of each run, Pallas kernels for 0% -> 0%
where the time goes in v1:
time: 1430 us; the launch traced here: 1420 us
  waiting for transfers between devices  890 us (62%)
  other arithmetic  369 us (26%)
  local copies, waits for them, and re-layouts  49.2 us (3%)
  matrix products  42.5 us (3%)
  starting transfers between devices  36.1 us (3%)
  between operations  21.4 us (1%)
    psum x2, waiting for transfers between devices, on_device(): gram_a, gram_b = lax.psum((local_a, local_b), ('vox', 'col'))  515 us
    all_gather x3, waiting for transfers between devices, quotient(): parts = lax.all_gather(own, ('vox', 'col'))  352 us
    another operation x21, other arithmetic, project_pencil(): lower = jnp.linalg.cholesky(normed_b)  114 us
    another operation x18, other arithmetic, project_pencil(): factor = jnp.linalg.cholesky(matmul(iterate.T, iterate))  74.7 us
    another operation x12, other arithmetic, lower_solve(): return lax.linalg.triangular_solve(lower, rhs, left_side=True, lower=True)  62.8 us
    another operation x5, other arithmetic, upper_solve(): lax.linalg.triangular_solve(lower, rhs, left_side=True, lower=True, trans...  59.5 us
  transfers between devices with their start and end apart: 16, of which 12 were waited for; matrix products, arithmetic and copies ran while one was open for 2% of the time, Pallas kernels for 0%

profile of v1, /device:TPU:1, one launch (start us, length us, event | category | flops | bytes accessed | tf_op | source)
XLA Modules:
  0.0 1421.7 jit_solution(4915920932251080061)
XLA Ops:
  7.9 4.5 collective-permute-start
  14.1 4.1 all-to-all-start
  31.4 4.4 collective-permute-done.2
  38.1 4.5 multiply_subtract_fusion.3
  44.6 7.2 all-to-all-start.1
  51.8 6.5 all-to-all-done.1
  64.9 4.7 collective-permute-done.6
  73.5 116.6 %all-gather.7.cloned.1.call-done = f32[32768,128]{0,1:T(8,128)} async-done(((f32[128,128]{0,1:T(8,128)}), f32[32768,128]{0,1:T(8,128)}) %all-gather.7.cloned.1.call-update) | async-done | bytes 16777232 | tf_op jit(solution)/shard_map/all_gather | solution.py:105
  190.1 14.1 copy.147
  204.2 8.0 bitcast_reduce_fusion
  219.0 5.5 fusion.64
  229.6 4.4 fusion.89
  237.3 255.8 %all-reduce.14.cloned.1.call-done = (f32[384,384]{1,0:T(8,128)}, f32[384,384]{0,1:T(8,128)}) async-done(((f32[384,384]{1,0:T(8,128)}, f32[384,384]{0,1:T(8,128)}), (f32[384,384]{1,0:T(8,128)}, f32[384,384]{0,1:T(8,128)})) %all-reduce.14.cloned.1.call-update) | async-done | bytes 1179664 | tf_op jit(solution)/shard_map/psum | solution.py:154
  495.3 3.9 gather_fusion
  500.8 11.7 cholesky.310
  512.6 9.8 custom-call.40
  523.0 11.7 cholesky.329
  534.8 10.0 custom-call.41
  545.2 11.7 cholesky.348
  560.3 6.2 while.12
  566.5 29.7 %custom-call.47 = f32[3,128,128]{1,2,0:T(8,128)S(1)} custom-call(f32[3,128,128]{2,1,0:T(8,128)S(1)} %get-tuple-element.49), custom_call_target="InvertDiagBlocksLowerTriangular" | custom-call | tf_op jit(solution)/shard_map/triangular_solve/custom-call.8 | solution.py:45
  603.7 11.7 cholesky.361
  616.8 9.8 custom-call.44
  628.9 11.7 cholesky.372
  641.9 9.8 custom-call.45
  653.6 11.9 cholesky.383
  666.8 9.8 custom-call.46
  681.6 124.7 %all-gather.9.cloned.1.call-done = f32[32768,128]{1,0:T(8,128)} async-done(((f32[128,128]{1,0:T(8,128)}), f32[32768,128]{1,0:T(8,128)}) %all-gather.9.cloned.1.call-update) | async-done | bytes 16777232 | tf_op jit(solution)/shard_map/all_gather | solution.py:105
  806.4 6.6 reduce_sum.60
  826.8 4.4 fusion.39
  833.7 259.0 %all-reduce.12.cloned.1.call-done = (f32[384,384]{1,0:T(8,128)}, f32[384,384]{0,1:T(8,128)}) async-done(((f32[384,384]{1,0:T(8,128)}, f32[384,384]{0,1:T(8,128)}), (f32[384,384]{1,0:T(8,128)}, f32[384,384]{0,1:T(8,128)})) %all-reduce.12.cloned.1.call-update) | async-done | bytes 1179664 | tf_op jit(solution)/shard_map/psum | solution.py:154
  1095.0 3.7 gather_fusion.1
  1100.2 11.7 cholesky.396
  1112.0 9.8 custom-call.48
  1122.4 11.7 cholesky.415
  1135.5 10.2 custom-call.49
  1146.2 11.7 cholesky.434
  1160.6 6.4 while.13
  1166.9 29.7 %custom-call.55 = f32[3,128,128]{1,2,0:T(8,128)S(1)} custom-call(f32[3,128,128]{2,1,0:T(8,128)S(1)} %get-tuple-element.52), custom_call_target="InvertDiagBlocksLowerTriangular" | custom-call | tf_op jit(solution)/shard_map/triangular_solve/custom-call.8 | solution.py:45
  1204.1 11.7 cholesky.447
  1217.1 9.8 custom-call.52
  1229.0 11.7 cholesky.458
  1242.0 9.8 custom-call.53
  1253.7 11.9 cholesky.469
  1267.0 9.8 custom-call.54
  1282.2 13.4 all_to_all.57
  1296.3 111.2 %all-gather.11.cloned.1.call-done = f32[32768,128]{1,0:T(8,128)} async-done(((f32[128,128]{1,0:T(8,128)}), f32[32768,128]{1,0:T(8,128)}) %all-gather.11.cloned.1.call-update) | async-done | bytes 16777232 | tf_op jit(solution)/shard_map/all_gather | solution.py:105
  1407.4 6.6 reduce_sum.62
  (389 shorter events, 127.6 us)
Async XLA Ops:
  7.9 14.0 collective-permute-start
  14.1 10.6 all-to-all-start
  18.3 171.8 %all-gather.7.cloned.1.call-start = ((), (), s32[]{:S(2)}) async-start(), calls=%async_computation.3 | async-start | bytes 16842752 | tf_op jit(solution)/shard_map/all_gather | solution.py:105
  21.7 20.9 %copy-start.18 = (f32[2,256]{1,0:T(2,128)}, f32[2,256]{1,0:T(2,128)S(1)}, u32[]{:S(2)}) copy-start(f32[2,256]{1,0:T(2,128)S(1)} %mul.1121) | copy-start | bytes 6148
  21.7 20.9 %copy-start.20 = (f32[2,256]{1,0:T(2,128)}, f32[2,256]{1,0:T(2,128)S(1)}, u32[]{:S(2)}) copy-start(f32[2,256]{1,0:T(2,128)S(1)} %mul.1127) | copy-start | bytes 6148
  21.7 20.9 %copy-start.22 = (f32[2,256]{1,0:T(2,128)}, f32[2,256]{1,0:T(2,128)S(1)}, u32[]{:S(2)}) copy-start(f32[2,256]{1,0:T(2,128)S(1)} %mul.1073) | copy-start | bytes 6148
  21.7 20.9 %copy-start.24 = (f32[2,256]{1,0:T(2,128)}, f32[2,256]{1,0:T(2,128)S(1)}, u32[]{:S(2)}) copy-start(f32[2,256]{1,0:T(2,128)S(1)} %mul.1079) | copy-start | bytes 6148
  21.8 20.8 %copy-start.26 = (f32[2,256]{1,0:T(2,128)}, f32[2,256]{1,0:T(2,128)S(1)}, u32[]{:S(2)}) copy-start(f32[2,256]{1,0:T(2,128)S(1)} %mul.1085) | copy-start | bytes 6148
  21.8 20.8 %copy-start.28 = (f32[2,256]{1,0:T(2,128)}, f32[2,256]{1,0:T(2,128)S(1)}, u32[]{:S(2)}) copy-start(f32[2,256]{1,0:T(2,128)S(1)} %mul.1091) | copy-start | bytes 6148
  21.8 20.8 %copy-start.30 = (f32[2,256]{1,0:T(2,128)}, f32[2,256]{1,0:T(2,128)S(1)}, u32[]{:S(2)}) copy-start(f32[2,256]{1,0:T(2,128)S(1)} %mul.1097) | copy-start | bytes 6148
  21.8 20.8 %copy-start.32 = (f32[2,256]{1,0:T(2,128)}, f32[2,256]{1,0:T(2,128)S(1)}, u32[]{:S(2)}) copy-start(f32[2,256]{1,0:T(2,128)S(1)} %mul.1103) | copy-start | bytes 6148
  21.9 20.8 %copy-start.34 = (f32[2,256]{1,0:T(2,128)}, f32[2,256]{1,0:T(2,128)S(1)}, u32[]{:S(2)}) copy-start(f32[2,256]{1,0:T(2,128)S(1)} %mul.1133) | copy-start | bytes 6148
  21.9 20.8 %copy-start.36 = (f32[2,256]{1,0:T(2,128)}, f32[2,256]{1,0:T(2,128)S(1)}, u32[]{:S(2)}) copy-start(f32[2,256]{1,0:T(2,128)S(1)} %mul.1139) | copy-start | bytes 6148
  21.9 20.8 %copy-start.38 = (f32[2,256]{1,0:T(2,128)}, f32[2,256]{1,0:T(2,128)S(1)}, u32[]{:S(2)}) copy-start(f32[2,256]{1,0:T(2,128)S(1)} %slice_bitcast_fusion.24) | copy-start | bytes 6148
  25.0 6.4 collective-permute-start.1
  28.1 7.7 collective-permute-start.2
  30.1 12.6 copy-start.40
  30.1 12.6 copy-start.42
  30.1 12.6 copy-start.44
  30.1 12.6 copy-start.46
  30.1 12.6 copy-start.48
  30.1 12.6 copy-start.50
  30.2 12.6 copy-start.52
  30.2 12.6 copy-start.54
  30.2 12.6 copy-start.56
  30.2 12.6 copy-start.58
  30.2 12.6 copy-start.60
  30.2 12.6 copy-start.62
  44.6 13.7 all-to-all-start.1
  51.8 441.3 %all-reduce.14.cloned.1.call-start = ((), (), s32[]{:S(2)}) async-start(), calls=%async_computation.7 | async-start | bytes 2359296 | tf_op jit(solution)/shard_map/psum | solution.py:154
  58.5 6.4 collective-permute-start.5
  61.6 8.0 collective-permute-start.6
  64.9 139.3 %copy-start.10 = (f32[128,1,2,256]{3,2,0,1:T(2,128)}, f32[128,1,2,256]{3,2,0,1:T(2,128)S(1)}, u32[]{:S(2)}) copy-start(f32[128,1,2,256]{3,2,0,1:T(2,128)S(1)} %collective-permute-done.5) | copy-start | bytes 786436
  214.3 12.7 copy-start.13
  214.3 12.7 collective-permute-start.3
  216.3 10.7 collective-permute-start.4
  237.2 569.2 %all-gather.9.cloned.1.call-start = ((), (), s32[]{:S(2)}) async-start(), calls=%async_computation.4 | async-start | bytes 16842752 | tf_op jit(solution)/shard_map/all_gather | solution.py:105
  653.0 26.4 %copy-start.5 = (f32[128,512]{1,0:T(8,128)S(1)}, f32[128,512]{1,0:T(8,128)}, u32[]{:S(2)}) copy-start(f32[128,512]{1,0:T(8,128)} %copy-done.4) | copy-start | bytes 786436
  653.0 26.4 %copy-start.7 = (f32[128,512]{1,0:T(8,128)S(1)}, f32[128,512]{1,0:T(8,128)}, u32[]{:S(2)}) copy-start(f32[128,512]{1,0:T(8,128)} %copy-done.6) | copy-start | bytes 786436
  681.1 411.6 %all-reduce.12.cloned.1.call-start = ((), (), s32[]{:S(2)}) async-start(), calls=%async_computation.6 | async-start | bytes 2359296 | tf_op jit(solution)/shard_map/psum | solution.py:154
  681.6 149.7 %copy-start.8 = (f32[128,512]{1,0:T(8,128)}, f32[128,512]{1,0:T(8,128)S(1)}, u32[]{:S(2)}) copy-start(f32[128,512]{1,0:T(8,128)S(1)} %fusion.15) | copy-start | bytes 786436
  813.6 7.9 collective-permute-start.7
  816.8 7.7 collective-permute-start.8
  819.2 12.1 copy-start.14
  831.3 267.3 %copy-start.16 = (f32[128,512]{1,0:T(8,128)}, f32[128,512]{1,0:T(8,128)S(1)}, u32[]{:S(2)}) copy-start(f32[128,512]{1,0:T(8,128)S(1)} %multiply_subtract_fusion) | copy-start | bytes 786436
  833.6 573.8 %all-gather.11.cloned.1.call-start = ((), (), s32[]{:S(2)}) async-start(), calls=%async_computation.5 | async-start | bytes 16842752 | tf_op jit(solution)/shard_map/all_gather | solution.py:105
  1251.9 26.8 %copy-start.15 = (f32[128,512]{1,0:T(8,128)S(1)}, f32[128,512]{1,0:T(8,128)}, u32[]{:S(2)}) copy-start(f32[128,512]{1,0:T(8,128)} %copy-done.14) | copy-start | bytes 786436
  1253.1 27.3 %copy-start.9 = (f32[128,512]{1,0:T(8,128)S(1)}, f32[128,512]{1,0:T(8,128)}, u32[]{:S(2)}) copy-start(f32[128,512]{1,0:T(8,128)} %copy-done.8) | copy-start | bytes 786436
  (35 other events, 152.6 us)
Sparse Core Ops, SparseCore 0:
  44.0 146.0 all-gather.6
  237.3 255.7 all-reduce.13
  681.2 125.1 all-gather.8
  833.7 258.9 all-reduce.11
  1282.3 125.0 all-gather.10
